TPU v7x, 1024 devices: a whole 8x8x8 slice. The times are simulated.
1024 devices in a mesh: dp: 64 (over y, z_hi, core), tensor: 16 (over z_lo, x).
Axes of the slice: x: 8, y: 8, z: 8 (z_hi: 4, z_lo: 2; z = z_hi * 2 + z_lo), core: 2. Of those that a mesh axis runs over, the one named last changes fastest.
Arguments:
- tokens: bfloat16 [131072, 3072], P('dp', 'tensor'), may hold values from -6 to 6
- cotangent: bfloat16 [131072, 1024], P('dp'), may hold values from -8 to 8
- weight: bfloat16 [3072, 1024], P('tensor'), may hold values from -6 to 6
- momentum: bfloat16 [64, 3072, 1024], P('dp', 'tensor'), may hold values from -3.5 to 3.5
- threshold: int32 [1024], replicated, may hold values from 2 to 8
Outputs:
- key_values: bfloat16 [131072, 1024], P(('dp', 'tensor'))
- input_grad: bfloat16 [131072, 3072], P('dp', 'tensor')
- new_momentum: bfloat16 [64, 3072, 1024], P('dp', 'tensor')
- new_weight: bfloat16 [3072, 1024], P('tensor', 'dp')
All inputs are finite; a program needn't handle non-finite values.
Results may differ from a plain program's by a relative error of at most 0.017.
Values may be sent and summed in bfloat16 or wider, within the bound.
A program may use at most 32 MiB of HBM per device.

v0:
```python
import jax
import jax.numpy as jnp
from jax import lax
from jax.sharding import Mesh
from jax.sharding import PartitionSpec as P

D = 3072
TENSOR = ("tensor_0", "tensor_1")
DP_TENSOR = ("dp", "tensor_0", "tensor_1")


def own_block(parts, axes, turns):
    inside = parts.shape[1:]
    parts = parts.reshape(*(lax.axis_size(a) for a in axes), *inside)
    parts = jnp.moveaxis(parts, turns, range(len(axes))).reshape(-1, *inside)
    for k in turns:
        parts = lax.psum_scatter(parts, axes[k], scatter_dimension=0, tiled=True)
    return parts[0]


def cut_along(shard, dim, peers):
    lengths = shard.shape
    parts = shard.reshape(*lengths[:dim], peers, lengths[dim] // peers, *lengths[dim + 1 :])
    return jnp.moveaxis(parts, dim, 0)


def scatter_axes(shard, axes, turns, dim):
    peers = lax.axis_size(axes)
    return own_block(cut_along(shard, dim, peers), axes, turns)


def per_device(tokens, cotangent, weight, momentum, threshold):
    inverse = D ** (-0.5)
    key_values = (
        scatter_axes(
            (jnp.dot(tokens, weight, preferred_element_type=jnp.float32) * inverse).astype(
                jnp.bfloat16
            ),
            TENSOR,
            (1, 0),
            0,
        )
        .astype(jnp.float32)
        .astype(jnp.bfloat16)
    )
    input_grad = (
        lax.dot_general(
            cotangent, weight, (((1,), (1,)), ((), ())), preferred_element_type=jnp.float32
        )
        * inverse
    ).astype(jnp.bfloat16)
    gradient = (
        lax.dot_general(
            tokens, cotangent, (((0,), (0,)), ((), ())), preferred_element_type=jnp.float32
        )
        * inverse
    )
    fresh = (0.9 * momentum[0].astype(jnp.float32) + 0.1 * gradient).astype(jnp.bfloat16)
    column_share = weight.shape[1] // lax.axis_size("dp")
    arrived = lax.all_to_all(fresh[None], "dp", split_axis=2, concat_axis=0, tiled=True)
    votes = jnp.sum(jnp.clip(arrived.astype(jnp.float32) / 0.125, -1.0, 1.0), axis=0)
    first_column = lax.axis_index("dp") * column_share
    own_columns = lax.dynamic_slice_in_dim(weight, first_column, column_share, 1)
    own_limits = lax.dynamic_slice_in_dim(threshold, first_column, column_share, 0)
    update = jnp.clip(votes / own_limits.astype(jnp.float32)[None, :], -1.0, 1.0)
    new_weight = (own_columns.astype(jnp.float32) - 0.5 * update).astype(jnp.bfloat16)
    return (key_values, input_grad, fresh[None], new_weight)


def solution(mesh):
    split = Mesh(mesh.devices.reshape(mesh.shape["dp"], 2, 8), ("dp", "tensor_0", "tensor_1"))
    placed = (P("dp", TENSOR), P("dp", None), P(TENSOR, None), P("dp", TENSOR, None), P())
    return jax.shard_map(
        per_device,
        mesh=split,
        in_specs=placed,
        out_specs=(P(DP_TENSOR, None), P("dp", TENSOR), P("dp", TENSOR, None), P(TENSOR, "dp")),
        check_vma=False,
    )
```

profile of v0, /device:TPU:1, one launch (start us, length us, event | category | flops | bytes accessed | tf_op | source)
XLA Modules:
  0.0 121.5 jit_solution(3793715344188755608)
XLA Ops:
  7.2 0.0 reduce-scatter.3.cloned.1.call-start
  7.2 1.1 copy-done
  8.3 2.3 %multiply_convert_fusion = bf16[2048,1024]{1,0:T(8,128)(2,1)S(1)} fusion(bf16[2048,192]{0,1:T(8,128)(2,1)S(1)} %copy-done, bf16[192,1024]{1,0:T(8,128)(2,1)} %param.7), kind=kOutput, calls=%fused_computation | convolution fusion | flops 809500672 | bytes 5373952 | tf_op jit(solution)/shard_map/dot_general | solution.py:36
  10.6 2.4 %copy.14 = bf16[8,2,128,1024]{3,2,1,0:T(8,128)(2,1)} copy(bf16[8,2,128,1024]{3,2,0,1:T(8,128)(2,1)S(1)} %bitcast.19) | data formatting | bytes 8388608 | tf_op jit(solution)/shard_map/transpose | solution.py:15
  13.0 0.0 reduce-scatter.3.cloned.1.call-update
  13.0 1.0 copy-done.3
  14.0 3.2 %fusion.3 = bf16[1,192,1024]{2,1,0:T(8,128)(2,1)S(1)} fusion(bf16[2048,192]{0,1:T(8,128)(2,1)S(1)} %copy-done, bf16[2048,1024]{1,0:T(8,128)(2,1)} %param.6, bf16[1,192,1024]{2,1,0:T(8,128)(2,1)S(1)} %copy-done.3), kind=kOutput, calls=%fused_computation.6 | convolution fusion | flops 806289408 | bytes 5767168 | tf_op jit(solution)/shard_map/dot_general | solution.py:53
  17.2 0.8 copy.16
  18.1 0.5 broadcast.25
  18.6 4.0 %reduce.3 = bf16[1024,192]{1,0:T(8,128)(2,1)S(1)} reduce(bf16[1024,1,192]{2,1,0:T(2,128)(2,1)S(1)} %bitcast.20, bf16[]{:T(256)} %broadcast.25), dimensions={1}, to_apply=%bitcast.10.reduce_sub_computation | reduce | bytes 786434
  22.6 1.3 %reshape.29 = bf16[64,2,1536]{2,1,0:T(2,128)(2,1)} reshape(bf16[1024,192]{1,0:T(8,128)(2,1)S(1)} %reduce.3) | data formatting | bytes 786432
  24.0 23.5 %all-to-all-start = ((bf16[64,2,1536]{2,1,0:T(2,128)(2,1)}), bf16[64,2,1536]{2,1,0:T(2,128)(2,1)S(1)}, u32[]{:S(2)}, u32[]{:S(2)}) async-start(bf16[64,2,1536]{2,1,0:T(2,128)(2,1)} %reshape.29), calls=%async_computation.2 | async-start | bytes 786432 | tf_op jit(solution)/shard_map/all_to_all | solution.py:60
  47.5 0.0 reduce-scatter.5.cloned.1.call-start
  47.6 37.7 %reduce-scatter.3.cloned.1.call-done = bf16[2,128,1024]{2,1,0:T(8,128)(2,1)} async-done(((bf16[16,128,1024]{2,1,0:T(8,128)(2,1)}), bf16[2,128,1024]{2,1,0:T(8,128)(2,1)}) %reduce-scatter.3.cloned.1.call-update) | async-done | bytes 524304 | tf_op jit(solution)/shard_map/reduce_scatter | solution.py:17
  85.3 0.0 reduce-scatter.5.cloned.1.call-update
  85.3 0.1 constant_dynamic-slice_fusion
  85.4 0.1 copy.18
  85.5 0.8 dynamic-slice_convert_fusion
  86.3 4.6 %fusion = bf16[2048,192]{0,1:T(8,128)(2,1)} fusion(bf16[2048,1024]{1,0:T(8,128)(2,1)} %param.6, bf16[192,1024]{1,0:T(8,128)(2,1)S(1)} %copy-done.2), kind=kOutput, calls=%fused_computation.2 | convolution fusion | flops 806092800 | bytes 5373952 | tf_op jit(solution)/shard_map/dot_general | solution.py:47
  90.9 0.7 reshape.30
  91.6 0.1 multiply_clamp_fusion
  91.7 0.1 reduce.2
  91.9 0.7 subtract_convert_fusion
  92.5 22.1 %reduce-scatter.5.cloned.1.call-done = bf16[1,128,1024]{2,1,0:T(8,128)(2,1)} async-done(((bf16[2,128,1024]{2,1,0:T(8,128)(2,1)}), bf16[1,128,1024]{2,1,0:T(8,128)(2,1)}) %reduce-scatter.5.cloned.1.call-update) | async-done | bytes 262160 | tf_op jit(solution)/shard_map/reduce_scatter | solution.py:17
  (7 shorter events, 0.0 us)
Async XLA Ops:
  7.2 1.1 copy-start
  7.2 78.1 %reduce-scatter.3.cloned.1.call-start = ((), (), s32[]{:S(2)}) async-start(), calls=%async_computation.3 | async-start | bytes 4718592 | tf_op jit(solution)/shard_map/reduce_scatter | solution.py:17
  13.0 1.0 copy-start.3
  14.0 71.3 %copy-start.2 = (bf16[192,1024]{1,0:T(8,128)(2,1)S(1)}, bf16[192,1024]{1,0:T(8,128)(2,1)}, u32[]{:S(2)}) copy-start(bf16[192,1024]{1,0:T(8,128)(2,1)} %param.7) | copy-start | bytes 1179652
  17.2 73.7 %copy-start.1 = (bf16[1,192,1024]{2,1,0:T(8,128)(2,1)}, bf16[1,192,1024]{2,1,0:T(8,128)(2,1)S(1)}, u32[]{:S(2)}) copy-start(bf16[1,192,1024]{2,1,0:T(8,128)(2,1)S(1)} %fusion.3) | copy-start | bytes 1179652
  24.0 66.9 %all-to-all-start = ((bf16[64,2,1536]{2,1,0:T(2,128)(2,1)}), bf16[64,2,1536]{2,1,0:T(2,128)(2,1)S(1)}, u32[]{:S(2)}, u32[]{:S(2)}) async-start(bf16[64,2,1536]{2,1,0:T(2,128)(2,1)} %reshape.29), calls=%async_computation.2 | async-start | bytes 786432 | tf_op jit(solution)/shard_map/all_to_all | solution.py:60
  47.5 67.1 %reduce-scatter.5.cloned.1.call-start = ((), (), s32[]{:S(2)}) async-start(), calls=%async_computation.4 | async-start | bytes 786432 | tf_op jit(solution)/shard_map/reduce_scatter | solution.py:17
Sparse Core Ops, SparseCore 0:
  13.1 72.1 reduce-scatter.2
  89.2 25.3 reduce-scatter.4
where the time goes:
time: 122 us; the launch traced here: 121 us
  waiting for transfers between devices  59.9 us (49%)
  starting transfers between devices  23.6 us (19%)
  between operations  14.1 us (12%)
  matrix products  10.1 us (8%)
  local copies, waits for them, and re-layouts  8.04 us (7%)
  other arithmetic  5.73 us (5%)
    reduce_scatter x2, waiting for transfers between devices, own_block(): parts = lax.psum_scatter(parts, axes[k], scatter_dimension=0, tiled=True)  59.8 us
    all_to_all x1, starting transfers between devices, per_device(): lax.all_to_all(fresh[None], 'dp', split_axis=2, concat_axis=0, tiled=True)  23.5 us
    unnamed x12, local copies, waits for them, and re-layouts  4.72 us
    dot_general x1, matrix products, per_device(): lax.dot_general(cotangent, weight, (((1,), (1,)), ((), ())), preferred_el...  4.6 us
    unnamed x1, other arithmetic  4.03 us
    dot_general x1, matrix products, per_device(): lax.dot_general(tokens, cotangent, (((0,), (0,)), ((), ())), preferred_el...  3.24 us
  transfers between devices with their start and end apart: 3, of which 2 were waited for; matrix products, arithmetic and copies ran while one was open for 14% of the time, Pallas kernels for 0%

commit v1 on v0

v1 whole, which is shorter than its diff:
```python
import jax
import jax.numpy as jnp
from jax import lax
from jax.experimental import pallas as pl
from jax.experimental.pallas import tpu as pltpu
from jax.sharding import PartitionSpec as P

D = 3072
INVERSE = D ** (-0.5)
MESH = pl.DeviceIdType.MESH
F32 = jnp.float32
BF16 = jnp.bfloat16

NX, NY, NZ = 8, 8, 4
FEAT, ROWS, COLS = 192, 2048, 1024
HALF = COLS // 2
AHEAD = (4, 3, 5, 2, 6, 1, 7, 0)
SLOT = {d: s for s, d in enumerate(AHEAD)}


def place():
    dp, tensor = lax.axis_index("dp"), lax.axis_index("tensor")
    return dp // 8, (dp // 2) % 4, dp % 2, tensor // 8, tensor % 8


def device(y, z_hi, core, z_lo, x):
    return (y * 8 + z_hi * 2 + core, z_lo * 8 + x)


def remote(src, dst, sems, i, peer):
    send, recv = sems
    return pltpu.make_async_remote_copy(
        src_ref=src,
        dst_ref=dst,
        send_sem=send.at[i],
        recv_sem=recv.at[i],
        device_id=peer,
        device_id_type=MESH,
    )


def clipped(m):
    return jnp.clip(m.astype(F32) * 8.0, -1.0, 1.0)


def main_kernel(
    tok, cot, w, mom,
    kv, ig, fresh, votes,
    tf, tt, ww, cv, mv, fv, gv, own, ring_out, ring_in, kvv, yin, zout, zin, vv,
    local, wsend, wrecv, tsend, trecv, xsend, xrecv, ysend, yrecv, zsend, zrecv,
):
    y, zh, c, zl, x = place()
    right = device(y, zh, c, zl, (x + 1) % NX)
    left = device(y, zh, c, zl, (x + NX - 1) % NX)
    pair = device(y, zh, c, 1 - zl, x)
    outer = device(y, (zh + 3 - 2 * zl) % NZ, c, 1 - zl, x)
    y_peers = [device((y + d) % NY, zh, c, zl, x) for d in range(1, NY)]
    z_peers = [device(y, (zh + d) % NZ, c, zl, x) for d in range(1, NZ)]

    barrier = pltpu.get_barrier_semaphore()
    peers = [right, left, pair, outer] + y_peers + z_peers
    for p in peers:
        pl.semaphore_signal(barrier, inc=1, device_id=p, device_id_type=MESH)

    mine = pl.multiple_of(zl * 1024, 1024)
    theirs = pl.multiple_of((1 - zl) * 1024, 1024)
    loads = [
        pltpu.make_async_copy(tok.at[:, pl.ds(mine, 1024)], tt.at[pl.ds(0, FEAT)], local.at[0]),
        pltpu.make_async_copy(w, ww.at[pl.ds(0, FEAT)], local.at[1]),
        pltpu.make_async_copy(tok, tf, local.at[2]),
        pltpu.make_async_copy(mom, mv, local.at[3]),
        pltpu.make_async_copy(cot, cv, local.at[4]),
    ]
    for load in loads:
        load.start()

    pl.semaphore_wait(barrier, len(peers))

    def piece(d):
        return pl.multiple_of(((x + d) % NX) * 128, 128)

    token_copies = {}

    def send_tokens(d):
        token_copies[d] = remote(
            tok.at[:, pl.ds(pl.multiple_of(theirs + piece(d), 128), 128)],
            tt.at[pl.ds(FEAT, FEAT), pl.ds(piece(d), 128)],
            (tsend, trecv), SLOT[d], pair,
        )
        token_copies[d].start()

    weight_copies = [
        remote(w.at[:, pl.ds(h * HALF, HALF)], ww.at[pl.ds(FEAT, FEAT), pl.ds(h * HALF, HALF)],
               (wsend, wrecv), h, to)
        for h, to in enumerate((pair, outer))
    ]
    weight_copies[1].start()
    send_tokens(4)
    weight_copies[0].start()
    for d in AHEAD[1:]:
        send_tokens(d)

    loads[2].wait()
    loads[3].wait()
    loads[4].wait()

    def grad_step(i, _):
        at = pl.ds(pl.multiple_of(i * 256, 256), 256)
        grad = lax.dot_general(tf[...], cv[:, at], (((1,), (0,)), ((), ())), preferred_element_type=F32)
        fv[:, at] = (0.9 * mv[:, at].astype(F32) + 0.1 * (grad * INVERSE)).astype(BF16)
        return _

    lax.fori_loop(0, COLS // 256, grad_step, 0)
    y_copies = [
        remote(fv.at[:, pl.ds(pl.multiple_of(((y + d) % NY) * 128, 128), 128)], yin.at[d - 1],
               (ysend, yrecv), d - 1, y_peers[d - 1])
        for d in range(1, NY)
    ]
    for q in y_copies:
        q.start()
    stores = [pltpu.make_async_copy(fv, fresh, local.at[5])]
    stores[0].start()

    loads[0].wait()
    loads[1].wait()
    for q in weight_copies:
        q.wait_recv()

    def own_partial(d):
        token_copies[d].wait_recv()
        rows = tt[:, pl.ds(piece(d), 128)]
        for h in range(2):
            cols = pl.ds(h * HALF, HALF)
            own[SLOT[d], :, cols] = INVERSE * lax.dot_general(
                rows, ww[:, cols], (((0,), (0,)), ((), ())), preferred_element_type=F32
            )

    messages = {}

    def owner(way, k):
        ahead = 4 - (k + 1) // 2
        return ahead if way == 0 else (NX - ahead) % NX

    def half(way, k):
        return pl.ds(((k + way) % 2) * HALF, HALF)

    def send_sum(way, k):
        total = own[SLOT[owner(way, k)], :, half(way, k)]
        if k >= 2:
            messages[way, k - 2].wait_recv()
            total = total + ring_in[way * 7 + k - 2].astype(F32)
        ring_out[way * 7 + k] = total.astype(BF16)
        messages[way, k] = remote(ring_out.at[way * 7 + k], ring_in.at[way * 7 + k], (xsend, xrecv),
                                  way * 7 + k, right if way == 0 else left)
        messages[way, k].start()

    def input_grad_part(first, last):
        def step(i, _):
            at = pl.ds(pl.multiple_of(i * 256, 256), 256)
            gv[:, at] = (
                lax.dot_general(ww[pl.ds(0, FEAT)], cv[at, :], (((1,), (1,)), ((), ())),
                                preferred_element_type=F32) * INVERSE
            ).astype(BF16)
            return _

        lax.fori_loop(first, last, step, 0)

    own_partial(4)
    for way in range(2):
        send_sum(way, 0)
    own_partial(3)
    send_sum(0, 1)
    own_partial(5)
    send_sum(1, 1)
    input_grad_part(0, 4)
    for way in range(2):
        send_sum(way, 2)
    own_partial(2)
    own_partial(6)
    for way in range(2):
        send_sum(way, 3)
    input_grad_part(4, 8)
    stores.append(pltpu.make_async_copy(gv, ig, local.at[6]))
    stores[1].start()
    for way in range(2):
        send_sum(way, 4)
    own_partial(1)
    own_partial(7)
    for way in range(2):
        send_sum(way, 5)
    own_partial(0)
    for way in range(2):
        send_sum(way, 6)

    my_block = pl.ds(pl.multiple_of(y * 128, 128), 128)
    total = clipped(fv[:, my_block])
    for d in range(1, NY):
        y_copies[d - 1].wait_recv()
        total = total + clipped(yin[d - 1])
    zout[...] = total.T
    z_copies = [
        remote(zout.at[pl.ds(pl.multiple_of(((zh + d) % NZ) * 32, 32), 32)], zin.at[d - 1],
               (zsend, zrecv), d - 1, z_peers[d - 1])
        for d in range(1, NZ)
    ]
    for q in z_copies:
        q.start()

    for k in (5, 6):
        for way in range(2):
            messages[way, k].wait_recv()
    for h in range(2):
        cols = pl.ds(h * HALF, HALF)
        from_left, from_right = ring_in[6 - h], ring_in[7 + 5 + h]
        kvv[:, cols] = (own[SLOT[0], :, cols] + from_left.astype(F32) + from_right.astype(F32)).astype(BF16)
    stores.append(pltpu.make_async_copy(kvv, kv, local.at[7]))
    stores[2].start()

    part = zout[pl.ds(pl.multiple_of(zh * 32, 32), 32), :]
    for d in range(1, NZ):
        z_copies[d - 1].wait_recv()
        part = part + zin[d - 1]
    vv[...] = part
    stores.append(pltpu.make_async_copy(vv, votes, local.at[8]))
    stores[3].start()

    for q in weight_copies + [token_copies[d] for d in AHEAD] + y_copies + z_copies:
        q.wait_send()
    for way in range(2):
        for k in range(7):
            messages[way, k].wait_send()
    for q in stores:
        q.wait()


def last_kernel(votes, w, thr, out, wv, wt, tt, arrived, local, send, recv):
    y, zh, c, zl, x = place()
    other = device(y, zh, 1 - c, zl, x)
    barrier = pltpu.get_barrier_semaphore()
    pl.semaphore_signal(barrier, inc=1, device_id=other, device_id_type=MESH)
    block = pl.ds(pl.multiple_of(y * 128, 128), 128)
    load = pltpu.make_async_copy(w.at[:, block], wv, local.at[0])
    load.start()
    limits = jnp.broadcast_to(thr[pl.ds(y, 1), :].astype(F32), (8, 128))
    tt[...] = limits.T
    pl.semaphore_wait(barrier, 1)
    copy = remote(votes.at[pl.ds(pl.multiple_of((1 - c) * 16, 16), 16)], arrived, (send, recv), 0, other)
    copy.start()
    load.wait()
    wt[...] = wv[...].astype(F32).T
    mine = pl.ds(pl.multiple_of(zh * 32 + c * 16, 16), 16)
    own_w = wt[mine, :]
    own_limits = tt[mine, 0:1]
    copy.wait_recv()
    total = votes[pl.ds(pl.multiple_of(c * 16, 16), 16), :] + arrived[...]
    out[...] = (own_w - 0.5 * jnp.clip(total / own_limits, -1.0, 1.0)).astype(BF16)
    copy.wait_send()


ANY = pl.BlockSpec(memory_space=pl.ANY)
VMEM = pl.BlockSpec(memory_space=pltpu.VMEM)
DMA = pltpu.SemaphoreType.DMA


def per_device(tokens, cotangent, weight, momentum, threshold):
    shape = jax.ShapeDtypeStruct
    kv, ig, fresh, votes = pl.pallas_call(
        main_kernel,
        out_shape=(
            shape((128, COLS), BF16),
            shape((FEAT, ROWS), BF16),
            shape((FEAT, COLS), BF16),
            shape((32, FEAT), F32),
        ),
        in_specs=[ANY] * 4,
        out_specs=[ANY] * 4,
        scratch_shapes=[
            pltpu.VMEM((FEAT, ROWS), BF16),
            pltpu.VMEM((2 * FEAT, 1024), BF16),
            pltpu.VMEM((2 * FEAT, COLS), BF16),
            pltpu.VMEM((ROWS, COLS), BF16),
            pltpu.VMEM((FEAT, COLS), BF16),
            pltpu.VMEM((FEAT, COLS), BF16),
            pltpu.VMEM((FEAT, ROWS), BF16),
            pltpu.VMEM((NX, 128, COLS), F32),
            pltpu.VMEM((14, 128, HALF), BF16),
            pltpu.VMEM((14, 128, HALF), BF16),
            pltpu.VMEM((128, COLS), BF16),
            pltpu.VMEM((NY - 1, FEAT, 128), BF16),
            pltpu.VMEM((128, FEAT), F32),
            pltpu.VMEM((NZ - 1, 32, FEAT), F32),
            pltpu.VMEM((32, FEAT), F32),
            DMA((9,)),
            DMA((2,)), DMA((2,)),
            DMA((8,)), DMA((8,)),
            DMA((14,)), DMA((14,)),
            DMA((7,)), DMA((7,)),
            DMA((3,)), DMA((3,)),
        ],
        compiler_params=pltpu.CompilerParams(
            collective_id=0, has_side_effects=True, vmem_limit_bytes=48 * 2**20
        ),
        cost_estimate=pl.CostEstimate(flops=2_400_000_000, bytes_accessed=7_000_000, transcendentals=0),
        name="keys_and_votes",
    )(tokens.T, cotangent, weight, momentum[0])
    new_weight = pl.pallas_call(
        last_kernel,
        out_shape=shape((16, FEAT), BF16),
        in_specs=[VMEM, ANY, VMEM],
        out_specs=VMEM,
        scratch_shapes=[
            pltpu.VMEM((FEAT, 128), BF16),
            pltpu.VMEM((128, FEAT), F32),
            pltpu.VMEM((128, 8), F32),
            pltpu.VMEM((16, FEAT), F32),
            DMA((1,)),
            DMA((1,)), DMA((1,)),
        ],
        compiler_params=pltpu.CompilerParams(collective_id=1, has_side_effects=True),
        name="other_core",
    )(votes, weight, threshold.reshape(8, 128))
    return kv, ig.T, fresh[None], new_weight.T


def solution(mesh):
    return jax.shard_map(
        per_device,
        mesh=mesh,
        in_specs=(P("dp", "tensor"), P("dp", None), P("tensor", None), P("dp", "tensor", None), P()),
        out_specs=(P(("dp", "tensor"), None), P("dp", "tensor"), P("dp", "tensor", None), P("tensor", "dp")),
        check_vma=False,
    )
```

time: 122 us -> 65.1 us (0.53)
  waiting for transfers between devices: 59.9 us -> 0 us
  Pallas kernels: 0 us -> 56.6 us
  starting transfers between devices: 23.6 us -> 0 us
  between operations: 14.1 us -> 0.67 us
  matrix products: 10.1 us -> 0 us
  other arithmetic: 5.73 us -> 0 us
    reduce_scatter x2 -> x0, waiting for transfers between devices: 59.8 us -> none  [own_block(): parts = lax.psum_scatter(parts, axes[k], scatter_dimension=0, tiled=True)]
    pallas_call x0 -> x2, Pallas kernels: none -> 56.6 us  [the longest x1 49.6 us: per_device(): pl.pallas_call(main_kernel, out_shape=(shape((128, COLS), BF16), shape((F...]
    all_to_all x1 -> x0, starting transfers between devices: 23.5 us -> none  [per_device(): lax.all_to_all(fresh[None], 'dp', split_axis=2, concat_axis=0, tiled=True)]
    dot_general x3 -> x0, matrix products: 10.1 us -> none  [the longest x1 4.6 us: per_device(): lax.dot_general(cotangent, weight, (((1,), (1,)), ((), ())), preferred_el...]
    unnamed x1 -> x0, other arithmetic: 4.03 us -> none
    unnamed x12, local copies, waits for them, and re-layouts: 4.72 us -> 7.35 us
    transpose x1 -> x0, local copies, waits for them, and re-layouts: 2.38 us -> none  [own_block(): parts = jnp.moveaxis(parts, turns, range(len(axes))).reshape(-1, *inside)]
    convert_element_type x2 -> x0, other arithmetic: 1.46 us -> none  [the longest x1 0.78 us: per_device(): own_limits.astype(jnp.float32)[None, :]]
  transfers between devices with their start and end apart: 3 -> 0, of which waited for: 2 -> 0; matrix products, arithmetic and copies ran while one was open for 14% -> 0% of each run, Pallas kernels for 0% -> 0%
where the time goes in v1:
time: 65.1 us; the launch traced here: 64.6 us
  Pallas kernels  56.6 us (87%)
  local copies, waits for them, and re-layouts  7.35 us (11%)
  between operations  0.67 us (1%)
    pallas_call x1, Pallas kernels, per_device(): pl.pallas_call(main_kernel, out_shape=(shape((128, COLS), BF16), shape((F...  49.6 us
    unnamed x12, local copies, waits for them, and re-layouts  7.35 us
    pallas_call x1, Pallas kernels, per_device(): pl.pallas_call(last_kernel, out_shape=shape((16, FEAT), BF16), in_specs=[...  6.97 us

profile of v1, /device:TPU:1, one launch (start us, length us, event | category | flops | bytes accessed | tf_op | source)
XLA Modules:
  0.0 64.6 jit_solution(11843282889682567907)
XLA Ops:
  0.6 0.0 copy-start
  0.6 1.0 %copy-done = bf16[192,1024]{1,0:T(8,128)(2,1)S(1)} copy-done((bf16[192,1024]{1,0:T(8,128)(2,1)S(1)}, bf16[192,1024]{1,0:T(8,128)(2,1)}, u32[]{:S(2)}) %copy-start) | copy-done | bytes 393240
  1.6 0.0 copy-start.2
  1.6 1.1 %copy-done.2 = bf16[2048,192]{0,1:T(8,128)(2,1)S(1)} copy-done((bf16[2048,192]{0,1:T(8,128)(2,1)S(1)}, bf16[2048,192]{0,1:T(8,128)(2,1)}, u32[]{:S(2)}) %copy-start.2) | copy-done | bytes 786456
  2.8 0.0 copy-start.3
  2.8 1.0 %copy-done.3 = bf16[1,192,1024]{2,1,0:T(8,128)(2,1)S(1)} copy-done((bf16[1,192,1024]{2,1,0:T(8,128)(2,1)S(1)}, bf16[1,192,1024]{2,1,0:T(8,128)(2,1)}, u32[]{:S(2)}) %copy-start.3) | copy-done | bytes 393240
  3.8 49.6 %keys_and_votes.1 = (bf16[128,1024]{1,0:T(8,128)(2,1)S(1)}, bf16[192,2048]{1,0:T(8,128)(2,1)S(1)}, bf16[192,1024]{1,0:T(8,128)(2,1)S(1)}, f32[32,192]{1,0:T(8,128)S(1)}) custom-call(bf16[192,2048]{1,0:T(8,128)(2,1)S(1)} %bitcast.8, bf16[2048,1024]{1,0:T(8,128)(2,1)} %cot.1, bf16[192,1024]{1,0:T(8,128)(2,1)S(1)} %copy-done, bf16[192,1024]{1,0:T(8,128)(2,1)S(1)} %bitcast.9), custom_call_target="tpu_custom_call" | custom-call | flops 2400000000 | bytes 7000000 | tf_op jit(solution)/shard_map/keys_and_votes/pallas_call | solution.py:267
  53.4 0.0 copy-start.1
  53.4 0.6 copy-done.1
  54.0 7.0 %other_core.1 = bf16[16,192]{1,0:T(8,128)(2,1)} custom-call(f32[32,192]{1,0:T(8,128)} %copy-done.1, bf16[192,1024]{1,0:T(8,128)(2,1)} %w.3, s32[8,128]{1,0:T(8,128)} %bitcast.11), custom_call_target="tpu_custom_call" | custom-call | tf_op jit(solution)/shard_map/other_core/pallas_call | solution.py:306
  61.0 0.7 %copy.13 = bf16[128,1024]{1,0:T(8,128)(2,1)} copy(bf16[128,1024]{1,0:T(8,128)(2,1)S(1)} %get-tuple-element.16) | data formatting | bytes 524288
  61.7 0.9 %copy.14 = bf16[2048,192]{0,1:T(8,128)(2,1)} copy(bf16[2048,192]{0,1:T(8,128)(2,1)S(1)} %bitcast.6) | data formatting | bytes 1572864
  62.6 0.7 %copy.15 = bf16[1,192,1024]{2,1,0:T(8,128)(2,1)} copy(bf16[1,192,1024]{2,1,0:T(8,128)(2,1)S(1)} %bitcast.7) | data formatting | bytes 786432
  63.3 1.3 %copy.16 = bf16[192,16]{0,1:T(8,128)(2,1)} copy(bf16[192,16]{0,1:T(8,128)(2,1)} %bitcast.10) | data formatting | bytes 12288
Async XLA Ops:
  0.6 1.0 %copy-start = (bf16[192,1024]{1,0:T(8,128)(2,1)S(1)}, bf16[192,1024]{1,0:T(8,128)(2,1)}, u32[]{:S(2)}) copy-start(bf16[192,1024]{1,0:T(8,128)(2,1)} %w.3) | copy-start | bytes 1179652
  1.6 1.1 %copy-start.2 = (bf16[2048,192]{0,1:T(8,128)(2,1)S(1)}, bf16[2048,192]{0,1:T(8,128)(2,1)}, u32[]{:S(2)}) copy-start(bf16[2048,192]{0,1:T(8,128)(2,1)} %param.5) | copy-start | bytes 2359300
  2.8 1.0 %copy-start.3 = (bf16[1,192,1024]{2,1,0:T(8,128)(2,1)S(1)}, bf16[1,192,1024]{2,1,0:T(8,128)(2,1)}, u32[]{:S(2)}) copy-start(bf16[1,192,1024]{2,1,0:T(8,128)(2,1)} %param.8) | copy-start | bytes 1179652
  53.4 0.6 copy-start.1

commit v2 on v1

v2 whole, which is shorter than its diff:
```python
import jax
import jax.numpy as jnp
from jax import lax
from jax.experimental import pallas as pl
from jax.experimental.pallas import tpu as pltpu
from jax.sharding import PartitionSpec as P

D = 3072
INVERSE = D ** (-0.5)
MESH = pl.DeviceIdType.MESH
F32 = jnp.float32
BF16 = jnp.bfloat16

NX, NY, NZ = 8, 8, 4
LEADER = 2
FEAT, ROWS, COLS = 192, 2048, 1024
HALF, QUARTER = COLS // 2, COLS // 4
AHEAD = (4, 3, 5, 2, 6, 1, 7, 0)
SLOT = {d: s for s, d in enumerate(AHEAD)}


def place():
    dp, tensor = lax.axis_index("dp"), lax.axis_index("tensor")
    return dp // 8, (dp // 2) % 4, dp % 2, tensor // 8, tensor % 8


def device(y, z_hi, core, z_lo, x):
    return (y * 8 + z_hi * 2 + core, z_lo * 8 + x)


def remote(src, dst, sems, i, peer):
    send, recv = sems
    return pltpu.make_async_remote_copy(
        src_ref=src,
        dst_ref=dst,
        send_sem=send.at[i],
        recv_sem=recv.at[i],
        device_id=peer,
        device_id_type=MESH,
    )


def signal(semaphore, peer):
    pl.semaphore_signal(semaphore, inc=1, device_id=peer, device_id_type=MESH)


def clipped(m):
    return jnp.clip(m.astype(F32) * 8.0, -1.0, 1.0)


def main_kernel(
    tok, cot, w, mom, thr,
    kv, ig, fresh, new_w,
    tf, tt, ww, cv, mv, fv, gv, own, ring_out, ring_in, kvv, yin, zout, zin, wt, lt, nv,
    local, wsend, wrecv, tsend, trecv, xsend, xrecv, ysend, yrecv, zsend, zrecv, inside, others, ready,
):
    y, zh, c, zl, x = place()
    right = device(y, zh, c, zl, (x + 1) % NX)
    left = device(y, zh, c, zl, (x + NX - 1) % NX)
    pair = device(y, zh, c, 1 - zl, x)
    outer = device(y, (zh + 3 - 2 * zl) % NZ, c, 1 - zl, x)
    y_peers = [device((y + d) % NY, zh, c, zl, x) for d in range(1, NY)]
    z_peers = [device(y, (zh + d // 2) % NZ, (c + d) % 2, zl, x) for d in range(1, 2 * NZ)]

    barrier = pltpu.get_barrier_semaphore()
    from_leader = (x + NX - LEADER) % NX
    leads = from_leader == 0
    peers = [right, left, pair, outer]
    far = y_peers + z_peers
    for p in peers:
        signal(barrier, p)

    @pl.when(leads)
    def _():
        for p in far:
            signal(barrier, p)

    mine = pl.multiple_of(zl * 1024, 1024)
    theirs = pl.multiple_of((1 - zl) * 1024, 1024)
    loads = [
        pltpu.make_async_copy(tok.at[:, pl.ds(mine, 1024)], tt.at[pl.ds(0, FEAT)], local.at[0]),
        pltpu.make_async_copy(w, ww.at[pl.ds(0, FEAT)], local.at[1]),
        pltpu.make_async_copy(tok, tf, local.at[2]),
        pltpu.make_async_copy(mom, mv, local.at[3]),
        pltpu.make_async_copy(cot, cv, local.at[4]),
    ]
    for load in loads:
        load.start()

    @pl.when(leads)
    def _():
        pl.semaphore_wait(barrier, len(peers) + len(far))

    @pl.when(jnp.logical_not(leads))
    def _():
        pl.semaphore_wait(barrier, len(peers))

    def piece(d):
        return pl.multiple_of(((x + d) % NX) * 128, 128)

    token_copies = {}

    def send_tokens(d):
        token_copies[d] = remote(
            tok.at[:, pl.ds(pl.multiple_of(theirs + piece(d), 128), 128)],
            tt.at[pl.ds(FEAT, FEAT), pl.ds(piece(d), 128)],
            (tsend, trecv), SLOT[d], pair,
        )
        token_copies[d].start()

    weight_copies = [
        remote(w.at[:, pl.ds(q * QUARTER, QUARTER)], ww.at[pl.ds(FEAT, FEAT), pl.ds(q * QUARTER, QUARTER)],
               (wsend, wrecv), q, pair if q < 2 else outer)
        for q in range(4)
    ]
    send_tokens(4)
    for q in (2, 0, 3, 1):
        weight_copies[q].start()
    for d in AHEAD[1:]:
        send_tokens(d)

    loads[2].wait()
    loads[3].wait()
    loads[4].wait()

    def grad_step(i, _):
        at = pl.ds(pl.multiple_of(i * 512, 512), 512)
        grad = lax.dot_general(tf[...], cv[:, at], (((1,), (0,)), ((), ())), preferred_element_type=F32)
        fv[:, at] = (0.9 * mv[:, at].astype(F32) + 0.1 * (grad * INVERSE)).astype(BF16)
        return _

    lax.fori_loop(0, COLS // 512, grad_step, 0)
    y_copies = [
        remote(fv.at[:, pl.ds(pl.multiple_of(((y + d) % NY) * 128, 128), 128)], yin.at[d - 1],
               (ysend, yrecv), d - 1, y_peers[d - 1])
        for d in range(1, NY)
    ]
    stores = [pltpu.make_async_copy(fv, fresh, local.at[5])]
    stores[0].start()

    @pl.when((from_leader != 0) & (from_leader != 4) & (from_leader != 5))
    def _():
        pl.semaphore_wait(inside, 1)

    @pl.when((from_leader >= 1) & (from_leader <= 4))
    def _():
        signal(inside, left)

    @pl.when(from_leader >= 5)
    def _():
        signal(inside, right)

    @pl.when(leads)
    def _():
        pl.semaphore_wait(inside, 2)
        for p in far:
            signal(others, p)

    def leader_tells():
        @pl.when(leads)
        def _():
            pl.semaphore_wait(others, len(far))
            for d in range(1, NX):
                signal(ready, device(y, zh, c, zl, (x + d) % NX))

    def send_votes():
        @pl.when(jnp.logical_not(leads))
        def _():
            pl.semaphore_wait(ready, 1)

        for q in y_copies:
            q.start()

    loads[0].wait()
    loads[1].wait()

    def own_partial(d, q):
        cols = pl.ds(q * QUARTER, QUARTER)
        own[SLOT[d], :, cols] = INVERSE * lax.dot_general(
            tt[:, pl.ds(piece(d), 128)], ww[:, cols], (((0,), (0,)), ((), ())), preferred_element_type=F32
        )

    def own_partials(d):
        token_copies[d].wait_recv()
        for q in range(4):
            own_partial(d, q)

    messages = {}

    def quarter(way, m):
        return ((m // 2 + way) % 2) * 2 + m % 2

    def owner(way, m):
        ahead = 4 - (m // 2 + 1) // 2
        return ahead if way == 0 else (NX - ahead) % NX

    def send_sum(way, m):
        at = way * 14 + m
        total = own[SLOT[owner(way, m)], :, pl.ds(quarter(way, m) * QUARTER, QUARTER)]
        if m >= 4:
            messages[way, m - 4].wait_recv()
            total = total + ring_in[at - 4].astype(F32)
        ring_out[at] = total.astype(BF16)
        messages[way, m] = remote(ring_out.at[at], ring_in.at[at], (xsend, xrecv), at,
                                  right if way == 0 else left)
        messages[way, m].start()

    def send_step(k):
        for m in (2 * k, 2 * k + 1):
            for way in range(2):
                send_sum(way, m)

    def input_grad_part(first, last):
        def step(i, _):
            at = pl.ds(pl.multiple_of(i * 512, 512), 512)
            gv[:, at] = (
                lax.dot_general(ww[pl.ds(0, FEAT)], cv[at, :], (((1,), (1,)), ((), ())),
                                preferred_element_type=F32) * INVERSE
            ).astype(BF16)
            return _

        lax.fori_loop(first, last, step, 0)

    token_copies[4].wait_recv()
    for m in range(2):
        for way in (1, 0):
            q = quarter(way, m)
            weight_copies[q].wait_recv()
            own_partial(4, q)
            send_sum(way, m)
    own_partials(3)
    own_partials(5)
    send_step(1)
    input_grad_part(0, 2)
    send_step(2)
    leader_tells()
    own_partials(2)
    own_partials(6)
    send_step(3)
    send_votes()
    input_grad_part(2, 4)
    stores.append(pltpu.make_async_copy(gv, ig, local.at[6]))
    stores[1].start()
    send_step(4)
    own_partials(1)
    own_partials(7)
    send_step(5)
    own_partials(0)
    send_step(6)

    my_block = pl.ds(pl.multiple_of(y * 128, 128), 128)
    total = clipped(fv[:, my_block])
    for d in range(1, NY):
        y_copies[d - 1].wait_recv()
        total = total + clipped(yin[d - 1])
    zout[...] = total.T
    z_copies = [
        remote(zout.at[pl.ds(pl.multiple_of(((zh + d // 2) % NZ) * 32 + ((c + d) % 2) * 16, 16), 16)],
               zin.at[d - 1], (zsend, zrecv), d - 1, z_peers[d - 1])
        for d in range(1, 2 * NZ)
    ]
    for q in z_copies:
        q.start()

    arrived = {(way, quarter(way, m)): m for way in range(2) for m in range(10, 14)}
    for q in (2, 3, 0, 1):
        cols = pl.ds(q * QUARTER, QUARTER)
        total = own[SLOT[0], :, cols]
        for way in range(2):
            messages[way, arrived[way, q]].wait_recv()
            total = total + ring_in[way * 14 + arrived[way, q]].astype(F32)
        kvv[:, cols] = total.astype(BF16)
    stores.append(pltpu.make_async_copy(kvv, kv, local.at[7]))
    stores[2].start()

    own_columns = pl.ds(pl.multiple_of(zh * 32 + c * 16, 16), 16)
    wt[...] = ww[pl.ds(0, FEAT), my_block].astype(F32).T
    lt[...] = jnp.broadcast_to(thr[pl.ds(y, 1), :].astype(F32), (8, 128)).T
    part = zout[own_columns, :]
    for d in range(1, 2 * NZ):
        z_copies[d - 1].wait_recv()
        part = part + zin[d - 1]
    update = jnp.clip(part / lt[own_columns, 0:1], -1.0, 1.0)
    nv[...] = (wt[own_columns, :] - 0.5 * update).astype(BF16)
    stores.append(pltpu.make_async_copy(nv, new_w, local.at[8]))
    stores[3].start()

    for q in weight_copies + [token_copies[d] for d in AHEAD] + y_copies + z_copies:
        q.wait_send()
    for way in range(2):
        for m in range(14):
            messages[way, m].wait_send()
    for q in stores:
        q.wait()


def write_kernel(*refs):
    ins, outs, held, sems = refs[:4], refs[4:8], refs[8:12], refs[12]
    loads = [pltpu.make_async_copy(a, b, sems.at[i]) for i, (a, b) in enumerate(zip(ins, held))]
    stores = [pltpu.make_async_copy(a, b, sems.at[4 + i]) for i, (a, b) in enumerate(zip(held, outs))]
    for q in loads:
        q.start()
    for i in (3, 0, 2, 1):
        loads[i].wait()
        stores[i].start()
    for q in stores:
        q.wait()


ANY = pl.BlockSpec(memory_space=pl.ANY)
HBM = pl.BlockSpec(memory_space=pltpu.HBM)
VMEM = pl.BlockSpec(memory_space=pltpu.VMEM)
DMA = pltpu.SemaphoreType.DMA


def per_device(tokens, cotangent, weight, momentum, threshold):
    shape = jax.ShapeDtypeStruct
    results = pl.pallas_call(
        main_kernel,
        out_shape=(
            shape((128, COLS), BF16),
            shape((FEAT, ROWS), BF16),
            shape((FEAT, COLS), BF16),
            shape((16, FEAT), BF16),
        ),
        in_specs=[HBM] * 4 + [VMEM],
        out_specs=[ANY] * 4,
        scratch_shapes=[
            pltpu.VMEM((FEAT, ROWS), BF16),
            pltpu.VMEM((2 * FEAT, 1024), BF16),
            pltpu.VMEM((2 * FEAT, COLS), BF16),
            pltpu.VMEM((ROWS, COLS), BF16),
            pltpu.VMEM((FEAT, COLS), BF16),
            pltpu.VMEM((FEAT, COLS), BF16),
            pltpu.VMEM((FEAT, ROWS), BF16),
            pltpu.VMEM((NX, 128, COLS), F32),
            pltpu.VMEM((28, 128, QUARTER), BF16),
            pltpu.VMEM((28, 128, QUARTER), BF16),
            pltpu.VMEM((128, COLS), BF16),
            pltpu.VMEM((NY - 1, FEAT, 128), BF16),
            pltpu.VMEM((128, FEAT), F32),
            pltpu.VMEM((2 * NZ - 1, 16, FEAT), F32),
            pltpu.VMEM((128, FEAT), F32),
            pltpu.VMEM((128, 8), F32),
            pltpu.VMEM((16, FEAT), BF16),
            DMA((9,)),
            DMA((4,)), DMA((4,)),
            DMA((8,)), DMA((8,)),
            DMA((28,)), DMA((28,)),
            DMA((7,)), DMA((7,)),
            DMA((7,)), DMA((7,)),
            pltpu.SemaphoreType.REGULAR,
            pltpu.SemaphoreType.REGULAR,
            pltpu.SemaphoreType.REGULAR,
        ],
        compiler_params=pltpu.CompilerParams(
            collective_id=0, has_side_effects=True, vmem_limit_bytes=61 * 2**20
        ),
        cost_estimate=pl.CostEstimate(flops=2_400_000_000, bytes_accessed=7_000_000, transcendentals=0),
        name="keys_and_votes",
    )(tokens.T, cotangent, weight, momentum[0], threshold.reshape(8, 128))
    kv, ig, fresh, new_weight = pl.pallas_call(
        write_kernel,
        out_shape=tuple(shape(a.shape, a.dtype) for a in results),
        in_specs=[ANY] * 4,
        out_specs=[HBM] * 4,
        scratch_shapes=[pltpu.VMEM(a.shape, a.dtype) for a in results] + [DMA((8,))],
        compiler_params=pltpu.CompilerParams(vmem_limit_bytes=61 * 2**20),
        name="write_results",
    )(*results)
    return kv, ig.T, fresh[None], new_weight.T


def solution(mesh):
    return jax.shard_map(
        per_device,
        mesh=mesh,
        in_specs=(P("dp", "tensor"), P("dp", None), P("tensor", None), P("dp", "tensor", None), P()),
        out_specs=(P(("dp", "tensor"), None), P("dp", "tensor"), P("dp", "tensor", None), P("tensor", "dp")),
        check_vma=False,
    )
```

time: 65.1 us -> 57.5 us (0.88)
  local copies, waits for them, and re-layouts: 7.35 us -> 0 us
  Pallas kernels: 56.6 us -> 55.9 us
    unnamed x12 -> x0, local copies, waits for them, and re-layouts: 7.35 us -> none
    pallas_call x1, Pallas kernels: 6.97 us -> 2.4 us  [per_device(): pl.pallas_call(write_kernel, out_shape=tuple((shape(a.shape, a.dtype) for...]
    pallas_call x1, Pallas kernels: 49.6 us -> 53.5 us  [per_device(): pl.pallas_call(main_kernel, out_shape=(shape((128, COLS), BF16), shape((F...]
where the time goes in v2:
time: 57.5 us; the launch traced here: 56.6 us
  Pallas kernels  55.9 us (97%)
  between operations  0.64 us (1%)
    pallas_call x1, Pallas kernels, per_device(): pl.pallas_call(main_kernel, out_shape=(shape((128, COLS), BF16), shape((F...  53.5 us
    pallas_call x1, Pallas kernels, per_device(): pl.pallas_call(write_kernel, out_shape=tuple((shape(a.shape, a.dtype) for...  2.4 us

profile of v2, /device:TPU:1, one launch (start us, length us, event | category | flops | bytes accessed | tf_op | source)
XLA Modules:
  0.0 56.6 jit_solution(4423141695682919439)
XLA Ops:
  0.6 53.5 %keys_and_votes.1 = (bf16[128,1024]{1,0:T(8,128)(2,1)}, bf16[192,2048]{1,0:T(8,128)(2,1)}, bf16[192,1024]{1,0:T(8,128)(2,1)}, bf16[16,192]{1,0:T(8,128)(2,1)}) custom-call(bf16[192,2048]{1,0:T(8,128)(2,1)} %bitcast.6, bf16[2048,1024]{1,0:T(8,128)(2,1)} %cot.1, bf16[192,1024]{1,0:T(8,128)(2,1)} %w.1, bf16[192,1024]{1,0:T(8,128)(2,1)} %bitcast.8, ...), custom_call_target="tpu_custom_call" | custom-call | flops 2400000000 | bytes 7000000 | tf_op jit(solution)/shard_map/keys_and_votes/pallas_call | solution.py:318
  54.2 2.4 %write_results.1 = (bf16[128,1024]{1,0:T(8,128)(2,1)}, bf16[192,2048]{1,0:T(8,128)(2,1)}, bf16[192,1024]{1,0:T(8,128)(2,1)}, bf16[16,192]{1,0:T(8,128)(2,1)}) custom-call(bf16[128,1024]{1,0:T(8,128)(2,1)} %get-tuple-element.12.refs_0_, bf16[192,2048]{1,0:T(8,128)(2,1)} %get-tuple-element.13.refs_1_, bf16[192,1024]{1,0:T(8,128)(2,1)} %get-tuple-element.14.refs_2_, ...), custom_call_target="tpu_custom_call" | custom-call | tf_op jit(solution)/shard_map/write_results/pallas_call | solution.py:362

commit v3 on v2

--- a/solution.py
+++ b/solution.py
@@ -52,28 +52,39 @@
     tok, cot, w, mom, thr,
     kv, ig, fresh, new_w,
     tf, tt, ww, cv, mv, fv, gv, own, ring_out, ring_in, kvv, yin, zout, zin, wt, lt, nv,
-    local, wsend, wrecv, tsend, trecv, xsend, xrecv, ysend, yrecv, zsend, zrecv, inside, others, ready,
+    local, wsend, wrecv, tsend, trecv, xsend, xrecv, ysend, yrecv, zsend, zrecv, inside, above, below, ready,
 ):
     y, zh, c, zl, x = place()
     right = device(y, zh, c, zl, (x + 1) % NX)
     left = device(y, zh, c, zl, (x + NX - 1) % NX)
     pair = device(y, zh, c, 1 - zl, x)
+    z = zh * 2 + zl
     outer = device(y, (zh + 3 - 2 * zl) % NZ, c, 1 - zl, x)
+    inner = (z > 0) & (z < 7)
+    feeds_end = (z == 1) | (z == 6)
     y_peers = [device((y + d) % NY, zh, c, zl, x) for d in range(1, NY)]
     z_peers = [device(y, (zh + d // 2) % NZ, (c + d) % 2, zl, x) for d in range(1, 2 * NZ)]
 
     barrier = pltpu.get_barrier_semaphore()
     from_leader = (x + NX - LEADER) % NX
     leads = from_leader == 0
-    peers = [right, left, pair, outer]
-    far = y_peers + z_peers
+    peers = [right, left, pair] + y_peers
     for p in peers:
         signal(barrier, p)
 
-    @pl.when(leads)
+    @pl.when(inner)
     def _():
-        for p in far:
-            signal(barrier, p)
+        signal(barrier, outer)
+
+    rank = zh * 2 + c
+
+    def for_ranks(higher, act):
+        for r in range(2 * NZ):
+            @pl.when(leads & ((r > rank) if higher else (r < rank)))
+            def _(r=r):
+                act(device(y, r // 2, r % 2, zl, x))
+
+    for_ranks(True, lambda p: signal(barrier, p))
 
     mine = pl.multiple_of(zl * 1024, 1024)
     theirs = pl.multiple_of((1 - zl) * 1024, 1024)
@@ -87,13 +98,7 @@
     for load in loads:
         load.start()
 
-    @pl.when(leads)
-    def _():
-        pl.semaphore_wait(barrier, len(peers) + len(far))
-
-    @pl.when(jnp.logical_not(leads))
-    def _():
-        pl.semaphore_wait(barrier, len(peers))
+    pl.semaphore_wait(barrier, len(peers) + inner.astype(jnp.int32) + leads.astype(jnp.int32) * rank)
 
     def piece(d):
         return pl.multiple_of(((x + d) % NX) * 128, 128)
@@ -113,9 +118,21 @@
                (wsend, wrecv), q, pair if q < 2 else outer)
         for q in range(4)
     ]
+    end_copies = [
+        pltpu.make_async_remote_copy(
+            src_ref=w.at[:, pl.ds(q * QUARTER, QUARTER)],
+            dst_ref=ww.at[pl.ds(FEAT, FEAT), pl.ds(q * QUARTER, QUARTER)],
+            send_sem=wsend.at[q + 2], recv_sem=wrecv.at[q], device_id=pair, device_id_type=MESH,
+        )
+        for q in (2, 3)
+    ]
     send_tokens(4)
     for q in (2, 0, 3, 1):
-        weight_copies[q].start()
+        if q < 2:
+            weight_copies[q].start()
+        else:
+            pl.when(inner)(weight_copies[q].start)
+            pl.when(feeds_end)(end_copies[q - 2].start)
     for d in AHEAD[1:]:
         send_tokens(d)
 
@@ -135,6 +152,8 @@
                (ysend, yrecv), d - 1, y_peers[d - 1])
         for d in range(1, NY)
     ]
+    for q in y_copies:
+        q.start()
     stores = [pltpu.make_async_copy(fv, fresh, local.at[5])]
     stores[0].start()
 
@@ -153,22 +172,47 @@
     @pl.when(leads)
     def _():
         pl.semaphore_wait(inside, 2)
-        for p in far:
-            signal(others, p)
+
+    for_ranks(False, lambda p: signal(above, p))
 
     def leader_tells():
+        @pl.when(leads & (rank < 2 * NZ - 1))
+        def _():
+            pl.semaphore_wait(above, 2 * NZ - 1 - rank)
+
+        for_ranks(True, lambda p: signal(below, p))
+
+        @pl.when(leads & (rank > 0))
+        def _():
+            pl.semaphore_wait(below, rank)
+
         @pl.when(leads)
         def _():
-            pl.semaphore_wait(others, len(far))
             for d in range(1, NX):
                 signal(ready, device(y, zh, c, zl, (x + d) % NX))
+
+    my_block = pl.ds(pl.multiple_of(y * 128, 128), 128)
+
+    def sum_votes():
+        total = clipped(fv[:, my_block])
+        for d in range(1, NY):
+            y_copies[d - 1].wait_recv()
+            total = total + clipped(yin[d - 1])
+        zout[...] = total.T
+
+    z_copies = [
+        remote(zout.at[pl.ds(pl.multiple_of(((zh + d // 2) % NZ) * 32 + ((c + d) % 2) * 16, 16), 16)],
+               zin.at[d - 1], (zsend, zrecv), d - 1, z_peers[d - 1])
+        for d in range(1, 2 * NZ)
+    ]
+
 
     def send_votes():
         @pl.when(jnp.logical_not(leads))
         def _():
             pl.semaphore_wait(ready, 1)
 
-        for q in y_copies:
+        for q in z_copies:
             q.start()
 
     loads[0].wait()
@@ -233,34 +277,21 @@
     send_step(1)
     input_grad_part(0, 2)
     send_step(2)
-    leader_tells()
     own_partials(2)
     own_partials(6)
+    sum_votes()
     send_step(3)
-    send_votes()
+    leader_tells()
     input_grad_part(2, 4)
     stores.append(pltpu.make_async_copy(gv, ig, local.at[6]))
     stores[1].start()
     send_step(4)
+    send_votes()
     own_partials(1)
     own_partials(7)
     send_step(5)
     own_partials(0)
     send_step(6)
-
-    my_block = pl.ds(pl.multiple_of(y * 128, 128), 128)
-    total = clipped(fv[:, my_block])
-    for d in range(1, NY):
-        y_copies[d - 1].wait_recv()
-        total = total + clipped(yin[d - 1])
-    zout[...] = total.T
-    z_copies = [
-        remote(zout.at[pl.ds(pl.multiple_of(((zh + d // 2) % NZ) * 32 + ((c + d) % 2) * 16, 16), 16)],
-               zin.at[d - 1], (zsend, zrecv), d - 1, z_peers[d - 1])
-        for d in range(1, 2 * NZ)
-    ]
-    for q in z_copies:
-        q.start()
 
     arrived = {(way, quarter(way, m)): m for way in range(2) for m in range(10, 14)}
     for q in (2, 3, 0, 1):
@@ -285,7 +316,11 @@
     stores.append(pltpu.make_async_copy(nv, new_w, local.at[8]))
     stores[3].start()
 
-    for q in weight_copies + [token_copies[d] for d in AHEAD] + y_copies + z_copies:
+    for q in weight_copies[2:]:
+        pl.when(inner)(q.wait_send)
+    for q in end_copies:
+        pl.when(feeds_end)(q.wait_send)
+    for q in weight_copies[:2] + [token_copies[d] for d in AHEAD] + y_copies + z_copies:
         q.wait_send()
     for way in range(2):
         for m in range(14):
@@ -344,11 +379,12 @@
             pltpu.VMEM((128, 8), F32),
             pltpu.VMEM((16, FEAT), BF16),
             DMA((9,)),
-            DMA((4,)), DMA((4,)),
+            DMA((6,)), DMA((4,)),
             DMA((8,)), DMA((8,)),
             DMA((28,)), DMA((28,)),
             DMA((7,)), DMA((7,)),
             DMA((7,)), DMA((7,)),
+            pltpu.SemaphoreType.REGULAR,
             pltpu.SemaphoreType.REGULAR,
             pltpu.SemaphoreType.REGULAR,
             pltpu.SemaphoreType.REGULAR,

time: 57.5 us -> 52.1 us (0.906); the launches traced: 56.6 us -> 51.9 us
  Pallas kernels: 55.9 us -> 51.3 us
    pallas_call x1, Pallas kernels: 53.5 us -> 48.9 us  [per_device(): pl.pallas_call(main_kernel, out_shape=(shape((128, COLS), BF16), shape((F...]
where the time goes in v3:
time: 52.1 us; the launch traced here: 51.9 us
  Pallas kernels  51.3 us (98%)
  between operations  0.64 us (1%)
    pallas_call x1, Pallas kernels, per_device(): pl.pallas_call(main_kernel, out_shape=(shape((128, COLS), BF16), shape((F...  48.9 us
    pallas_call x1, Pallas kernels, per_device(): pl.pallas_call(write_kernel, out_shape=tuple((shape(a.shape, a.dtype) for...  2.4 us

profile of v3, /device:TPU:1, one launch (start us, length us, event | category | flops | bytes accessed | tf_op | source)
XLA Modules:
  0.0 51.9 jit_solution(1239539238933176595)
XLA Ops:
  0.6 48.9 %keys_and_votes.1 = (bf16[128,1024]{1,0:T(8,128)(2,1)}, bf16[192,2048]{1,0:T(8,128)(2,1)}, bf16[192,1024]{1,0:T(8,128)(2,1)}, bf16[16,192]{1,0:T(8,128)(2,1)}) custom-call(bf16[192,2048]{1,0:T(8,128)(2,1)} %bitcast.6, bf16[2048,1024]{1,0:T(8,128)(2,1)} %cot.1, bf16[192,1024]{1,0:T(8,128)(2,1)} %w.1, bf16[192,1024]{1,0:T(8,128)(2,1)} %bitcast.8, ...), custom_call_target="tpu_custom_call" | custom-call | flops 2400000000 | bytes 7000000 | tf_op jit(solution)/shard_map/keys_and_votes/pallas_call | solution.py:353
  49.5 2.4 %write_results.1 = (bf16[128,1024]{1,0:T(8,128)(2,1)}, bf16[192,2048]{1,0:T(8,128)(2,1)}, bf16[192,1024]{1,0:T(8,128)(2,1)}, bf16[16,192]{1,0:T(8,128)(2,1)}) custom-call(bf16[128,1024]{1,0:T(8,128)(2,1)} %get-tuple-element.12.refs_0_, bf16[192,2048]{1,0:T(8,128)(2,1)} %get-tuple-element.13.refs_1_, bf16[192,1024]{1,0:T(8,128)(2,1)} %get-tuple-element.14.refs_2_, ...), custom_call_target="tpu_custom_call" | custom-call | tf_op jit(solution)/shard_map/write_results/pallas_call | solution.py:398

commit v4 on v3

--- a/solution.py
+++ b/solution.py
@@ -280,13 +280,13 @@
     own_partials(2)
     own_partials(6)
     sum_votes()
+    leader_tells()
     send_step(3)
-    leader_tells()
+    send_votes()
     input_grad_part(2, 4)
     stores.append(pltpu.make_async_copy(gv, ig, local.at[6]))
     stores[1].start()
     send_step(4)
-    send_votes()
     own_partials(1)
     own_partials(7)
     send_step(5)

time: 52.1 us -> 50.5 us (0.969)
  Pallas kernels: 51.3 us -> 49.6 us
    pallas_call x1, Pallas kernels: 48.9 us -> 47.3 us  [per_device(): pl.pallas_call(main_kernel, out_shape=(shape((128, COLS), BF16), shape((F...]
where the time goes in v4:
time: 50.5 us; the launch traced here: 50.3 us
  Pallas kernels  49.6 us (98%)
  between operations  0.64 us (1%)
    pallas_call x1, Pallas kernels, per_device(): pl.pallas_call(main_kernel, out_shape=(shape((128, COLS), BF16), shape((F...  47.3 us
    pallas_call x1, Pallas kernels, per_device(): pl.pallas_call(write_kernel, out_shape=tuple((shape(a.shape, a.dtype) for...  2.4 us

profile of v4, /device:TPU:1, one launch (start us, length us, event | category | flops | bytes accessed | tf_op | source)
XLA Modules:
  0.0 50.3 jit_solution(14159482027846339682)
XLA Ops:
  0.6 47.3 %keys_and_votes.1 = (bf16[128,1024]{1,0:T(8,128)(2,1)}, bf16[192,2048]{1,0:T(8,128)(2,1)}, bf16[192,1024]{1,0:T(8,128)(2,1)}, bf16[16,192]{1,0:T(8,128)(2,1)}) custom-call(bf16[192,2048]{1,0:T(8,128)(2,1)} %bitcast.6, bf16[2048,1024]{1,0:T(8,128)(2,1)} %cot.1, bf16[192,1024]{1,0:T(8,128)(2,1)} %w.1, bf16[192,1024]{1,0:T(8,128)(2,1)} %bitcast.8, ...), custom_call_target="tpu_custom_call" | custom-call | flops 2400000000 | bytes 7000000 | tf_op jit(solution)/shard_map/keys_and_votes/pallas_call | solution.py:353
  47.9 2.4 %write_results.1 = (bf16[128,1024]{1,0:T(8,128)(2,1)}, bf16[192,2048]{1,0:T(8,128)(2,1)}, bf16[192,1024]{1,0:T(8,128)(2,1)}, bf16[16,192]{1,0:T(8,128)(2,1)}) custom-call(bf16[128,1024]{1,0:T(8,128)(2,1)} %get-tuple-element.12.refs_0_, bf16[192,2048]{1,0:T(8,128)(2,1)} %get-tuple-element.13.refs_1_, bf16[192,1024]{1,0:T(8,128)(2,1)} %get-tuple-element.14.refs_2_, ...), custom_call_target="tpu_custom_call" | custom-call | tf_op jit(solution)/shard_map/write_results/pallas_call | solution.py:398
